TPU v7x, 32 devices: a whole 2x2x4 slice. The times are simulated.
32 devices in a mesh: groups: 2 (over x), tiles: 8 (over z, y), sub: 2 (over core).
Axes of the slice: x: 2, y: 2, z: 4, core: 2. Of those that a mesh axis runs over, the one named last changes fastest.
Arguments:
- density: float32 [768, 1536], P(('groups', 'tiles'), 'sub'), parts along dimension 0, may hold values from 0.8 to 1.2
- momentum: float32 [3, 768, 1536], P(None, ('groups', 'tiles'), 'sub'), parts along dimension 1, may hold values from -0.4 to 0.4
- stress: float32 [6, 768, 1536], P(None, ('groups', 'tiles'), 'sub'), parts along dimension 1, may hold values from -0.4 to 0.4
- red_density: float32 [768, 1536], P(('groups', 'tiles'), 'sub'), parts along dimension 0, may hold values from 0.1 to 0.8
- solid: int32 [768, 1536], P(('groups', 'tiles'), 'sub'), parts along dimension 0, may hold values 0 or 1
- widths: int32 [16], P('groups'), parts along dimension 0, may hold values from 1 to 3, 16 in all
Outputs:
- density_next: float32 [768, 1536], P(('groups', 'tiles'), 'sub'), parts along dimension 0
- momentum_next: float32 [3, 768, 1536], P(None, ('groups', 'tiles'), 'sub'), parts along dimension 1
- stress_next: float32 [6, 768, 1536], P(None, ('groups', 'tiles'), 'sub'), parts along dimension 1
- red_next: float32 [768, 1536], P(('groups', 'tiles'), 'sub'), parts along dimension 0
There are 2 independent parts, one for each index of `groups`. A program takes and returns all parts, laid end to end along the dimension named above; each array names one. Nothing has to cross between parts.
Inputs may be any that keep to these rules, and one draw needn't show every extreme that they name: Device k along tiles owns the tile columns from widths[0] + ... + widths[k-1] on, widths[k] of them, alike in every part of sub; they sum to 16, and one equals 3. 1 marks a solid cell, 0 a pore cell.
All inputs are finite; a program needn't handle non-finite values. No bound on the sum of `solid` on one device may be relied on, other than what follows from the above.
Results may differ from a plain program's by a relative error of at most 0.0003.
Values sent between devices are 32-bit elements; how exact they have to be, the bound alone decides.
No kernel may reach another device: no remote copies, remote signals or barrier semaphores. Data moves between devices by JAX's collectives and lax.ppermute only.
A program may use at most 64 MiB of HBM per device.

v0:
```python
import functools

import jax
import jax.numpy as jnp
from jax import lax
from jax.experimental import pallas as pl
from jax.experimental.pallas import tpu as pltpu
from jax.sharding import PartitionSpec as P

TILE = 16
STEPS = 2
RELAX_TIME = 0.8
SURFACE = 0.1
SEPARATION = 0.7

LANES = 128
SUBLANES = 8
FULL = 3
HALO = FULL + 1
FIELDS = 11
PLANES = FIELDS + 1
MOVED = 19
REDS = 5
RIM = 4
SLAB = HALO + 2 * RIM
OWN_TILES = SUBLANES - 2
END_COUNT = 1 + FULL * PLANES
END_ROWS = -(-END_COUNT * OWN_TILES // SUBLANES) * SUBLANES
HALF = LANES // 2
PAIRS = PLANES // 2
COLOUR_BLOCK = (8, 1)
COLLIDE_BLOCK = (2, 4)
ARRIVE_BLOCK = (8, 1)
VMEM = pl.BlockSpec(memory_space=pltpu.VMEM)
SMEM = pl.BlockSpec(memory_space=pltpu.SMEM)
ANY = pl.BlockSpec(memory_space=pl.ANY)
HBM = pl.BlockSpec(memory_space=pltpu.HBM)


def roll_lanes(values, amount):
    return pltpu.roll(values, amount % LANES, 2)


class Geometry:
    def __init__(self, info, own_tiles):
        live, first, last, sub_index = info[0], info[1], info[2], info[3]
        self.live = live
        self.low_row = jnp.where(first == 1, 0, -1000)
        self.high_row = jnp.where(last == 1, live, 1000)
        shape = (1, SUBLANES, LANES)
        lane = lax.broadcasted_iota(jnp.int32, shape, 2)
        tile = lax.broadcasted_iota(jnp.int32, shape, 1)
        depth = lane & (TILE - 1)
        self.z_low = depth == 0
        self.z_high = depth == TILE - 1
        low_part = sub_index == 0
        high_part = sub_index == 1
        self.y_low = (tile == 1) & (lane < TILE) & low_part
        self.y_high = (tile == own_tiles) & (lane >= LANES - TILE) & high_part
        own = (tile >= 1) & (tile <= own_tiles)
        self.domain = own | ((tile == own_tiles + 1) & low_part) | ((tile == 0) & high_part)
        self.first_lanes = lane < TILE
        self.last_lanes = lane >= LANES - TILE

    def from_low_y(self, values, depth_shift=0, below=None):
        if below is None:
            below = pltpu.roll(values, 1, 1)
        return roll_lanes(jnp.where(self.last_lanes, below, values), TILE + depth_shift)

    def from_high_y(self, values, depth_shift=0, above=None):
        if above is None:
            above = pltpu.roll(values, SUBLANES - 1, 1)
        return roll_lanes(jnp.where(self.first_lanes, above, values), -TILE + depth_shift)

    def from_low_z(self, values):
        return jnp.where(self.z_low, 0.0, roll_lanes(values, 1))

    def from_high_z(self, values):
        return jnp.where(self.z_high, 0.0, roll_lanes(values, -1))


def flat_rows(row, count, tile_offset=0):
    start = row * SUBLANES
    if not isinstance(start, int):
        start = pl.multiple_of(start, SUBLANES)
    return pl.ds(start + tile_offset, count * SUBLANES)


class Block:
    def __init__(self, geometry, spans, inner=False, store_rows=None):
        self.spans = spans
        self.store_rows = store_rows or [local for row, local, count in spans]
        rows = [row + extra for row, local, count in spans for extra in range(count)]
        if inner:
            self.x_low = self.x_high = None
            self.valid = geometry.domain
            self.kinds = [0]
            return
        shape = (1, SUBLANES, LANES)
        ids = jnp.concatenate([row + jnp.zeros(shape, jnp.int32) for row in rows], axis=0)
        self.x_low = ids == geometry.low_row
        self.x_high = ids == geometry.high_row - 1
        self.valid = geometry.domain & (ids >= geometry.low_row) & (ids < geometry.high_row)
        self.kinds = [
            jnp.where(row == geometry.low_row, 1, 0) + jnp.where(row == geometry.high_row - 1, 2, 0)
            for row in rows
        ]

    def load(self, ref, index, offset=0, tile_offset=0):
        parts = [
            ref[index, flat_rows(local + offset, count, tile_offset), :].reshape(
                count, SUBLANES, LANES
            )
            for row, local, count in self.spans
        ]
        return parts[0] if len(parts) == 1 else jnp.concatenate(parts, axis=0)

    def store(self, ref, index, values):
        done = 0
        for (row, local, count), target in zip(self.spans, self.store_rows):
            part = values[done : done + count].reshape(count * SUBLANES, LANES)
            ref[index, flat_rows(target, count), :] = part
            done += count

    def walls(self, walls, position):
        parts = [walls[position, flat_rows(kind, 1), :][None] for kind in self.kinds]
        return jnp.concatenate(parts, axis=0)


def fill_wall_table(walls, geometry):
    one = jnp.ones((1, SUBLANES, LANES), jnp.float32)
    up_y = jnp.where(geometry.y_high, 0.0, one)
    down_y = jnp.where(geometry.y_low, 0.0, one)
    up_z = jnp.where(geometry.z_high, 0.0, one)
    down_z = jnp.where(geometry.z_low, 0.0, one)
    sum_y, sum_z = up_y + down_y, up_z + down_z
    for kind, (up_x, down_x) in enumerate(((1.0, 1.0), (1.0, 0.0), (0.0, 1.0))):
        sum_x = up_x + down_x
        around_x = 2.0 + sum_y + sum_z
        total = 12.0 + 2.0 * (sum_x + sum_y + sum_z) + sum_x * (sum_y + sum_z) + sum_y * sum_z
        rows = (
            (up_x - down_x) * around_x,
            (up_y - down_y) * (2.0 + sum_x + sum_z),
            (up_z - down_z) * (2.0 + sum_x + sum_y),
            36.0 - total,
        )
        for position, row in enumerate(rows):
            walls[position, flat_rows(kind, 1), :] = row[0]


def colour_stage(block, geometry, fields, colours):
    density = block.load(fields, 0)
    red = block.load(fields, 10)
    colour = jnp.where(block.valid, 2.0 * red - density, 0.0)
    along_y = geometry.from_low_y(colour) + geometry.from_high_y(colour)
    along_z = geometry.from_low_z(colour) + geometry.from_high_z(colour)
    block.store(colours, 0, colour)
    block.store(colours, 1, 2.0 * colour + (along_y + along_z))
    block.store(colours, 2, along_y)
    block.store(colours, 3, along_z)


def collide_stage(block, geometry, fields, solids, colours, walls, moved, reds):
    relaxing = 1.0 - 1.0 / RELAX_TIME
    third = 1.0 / 3.0
    colour = block.load(colours, 0)
    doubled = 2.0 * colour + (block.load(colours, 0, -1) + block.load(colours, 0, 1))
    term_y = doubled + block.load(colours, 3)
    term_z = doubled + block.load(colours, 2)
    grad_x = block.load(colours, 1, 1) - block.load(colours, 1, -1)
    grad_y = geometry.from_high_y(term_y) - geometry.from_low_y(term_y)
    grad_z = geometry.from_high_z(term_z) - geometry.from_low_z(term_z)
    grad_x = (grad_x - block.walls(walls, 0) * colour) * (1.0 / 12.0)
    grad_y = (grad_y - block.walls(walls, 1) * colour) * (1.0 / 12.0)
    grad_z = (grad_z - block.walls(walls, 2) * colour) * (1.0 / 12.0)

    fluid = block.load(solids, PLANES - 1) == 0.0
    density = block.load(fields, 0)
    red = block.load(fields, 10)
    flux = [block.load(fields, 1 + axis) for axis in range(3)]
    stress = [block.load(fields, 4 + part) for part in range(6)]
    square_xx, square_yy, square_zz = grad_x * grad_x, grad_y * grad_y, grad_z * grad_z
    square = square_xx + square_yy + square_zz
    inverse = jnp.where(fluid, lax.rsqrt(1.0 + square), 0.0)
    strength = SURFACE * inverse
    keep = jnp.where(fluid, relaxing, 1.0)
    sign = jnp.where(fluid, 1.0, -1.0)
    trace = third * square
    surface = (
        square_xx - trace,
        square_yy - trace,
        square_zz - trace,
        grad_x * grad_y,
        grad_x * grad_z,
        grad_y * grad_z,
    )
    pairs = ((0, 0), (1, 1), (2, 2), (0, 1), (0, 2), (1, 2))
    second = [
        flux[a] * flux[b] + (keep * before + strength * addend)
        for (a, b), before, addend in zip(pairs, stress, surface)
    ]
    flux = [sign * part for part in flux]
    mixing = (SEPARATION * red) * (density - red) * inverse
    charge = [0.5 * part + mixing * grad for part, grad in zip(flux, (grad_x, grad_y, grad_z))]

    base = (density - 1.5 * (second[0] + second[1] + second[2])) * (1.0 / 36.0)
    run = [part * (1.0 / 12.0) for part in flux]
    own = [part * 0.125 for part in second[:3]]
    cross = [part * 0.25 for part in second[3:]]
    block.store(moved, 0, 12.0 * base)
    straight = [base + part for part in own]
    for axis in range(3):
        middle = 2.0 * straight[axis]
        swing = 2.0 * run[axis]
        block.store(moved, 1 + 2 * axis, middle + swing)
        block.store(moved, 2 + 2 * axis, middle - swing)
    for plane, (a, b) in enumerate(((0, 1), (0, 2), (1, 2))):
        middle = straight[a] + own[b]
        same, other = middle + cross[plane], middle - cross[plane]
        along, against = run[a] + run[b], run[a] - run[b]
        first = 7 + 4 * plane
        block.store(moved, first, same + along)
        block.store(moved, first + 1, same - along)
        block.store(moved, first + 2, other + against)
        block.store(moved, first + 3, other - against)

    scale = jnp.where(block.valid, 1.0 / 12.0, 0.0)
    red_base = red * (scale * third)
    red_run = [part * scale for part in charge]
    block.store(reds, 0, red_base)
    block.store(reds, 1, red_base + red_run[0])
    block.store(reds, 2, red_base - red_run[0])
    block.store(reds, 3, red_run[1])
    block.store(reds, 4, red_run[2])


def arrive_stage(block, geometry, walls, moved, reds, fields):
    third = 1.0 / 3.0
    own = [None] * MOVED

    def here(direction):
        if own[direction] is None:
            own[direction] = block.load(moved, direction)
        return own[direction]

    def arrived(direction, opposite, velocity):
        vel_x, vel_y, vel_z = velocity
        values = here(direction) if vel_x == 0 else block.load(moved, direction, -vel_x)
        if vel_y == 1:
            below = block.load(moved, direction, -vel_x, -1)
            values = geometry.from_low_y(values, vel_z, below)
        elif vel_y == -1:
            above = block.load(moved, direction, -vel_x, 1)
            values = geometry.from_high_y(values, vel_z, above)
        elif vel_z != 0:
            values = roll_lanes(values, vel_z)
        masks = []
        if vel_x != 0 and block.x_low is not None:
            masks.append(block.x_low if vel_x == 1 else block.x_high)
        if vel_y != 0:
            masks.append(geometry.y_low if vel_y == 1 else geometry.y_high)
        if vel_z != 0:
            masks.append(geometry.z_low if vel_z == 1 else geometry.z_high)
        if not masks:
            return values
        wall = functools.reduce(lambda one, two: one | two, masks)
        return jnp.where(wall, here(opposite), values)

    rest = here(0)
    sums, diffs = [], []
    for axis in range(3):
        velocity = [0, 0, 0]
        velocity[axis] = 1
        up = arrived(1 + 2 * axis, 2 + 2 * axis, velocity)
        velocity[axis] = -1
        down = arrived(2 + 2 * axis, 1 + 2 * axis, velocity)
        sums.append(up + down)
        diffs.append(up - down)
    total = rest + sums[0] + sums[1] + sums[2]
    cross = []
    for plane, (a, b) in enumerate(((0, 1), (0, 2), (1, 2))):
        first = 7 + 4 * plane
        parts = []
        for offset, (vel_a, vel_b) in enumerate(((1, 1), (-1, -1), (1, -1), (-1, 1))):
            velocity = [0, 0, 0]
            velocity[a], velocity[b] = vel_a, vel_b
            parts.append(arrived(first + offset, first + (offset ^ 1), velocity))
        same, other = parts[0] + parts[1], parts[2] + parts[3]
        along, against = parts[0] - parts[1], parts[2] - parts[3]
        both = same + other
        cross.append(same - other)
        total = total + both
        sums[a], sums[b] = sums[a] + both, sums[b] + both
        diffs[a], diffs[b] = diffs[a] + (along + against), diffs[b] + (along - against)
    shared = third * total
    block.store(fields, 0, total)
    for axis in range(3):
        block.store(fields, 1 + axis, diffs[axis])
        block.store(fields, 4 + axis, sums[axis] - shared - diffs[axis] * diffs[axis])
    for plane, (a, b) in enumerate(((0, 1), (0, 2), (1, 2))):
        block.store(fields, 7 + plane, cross[plane] - diffs[a] * diffs[b])

    red = block.load(reds, 0)
    red_x_up = block.load(reds, 1)
    red_y = block.load(reds, 3)
    red_z = block.load(reds, 4)
    from_x = block.load(reds, 1, -1) + block.load(reds, 2, 1)
    spread = 2.0 * red + from_x
    spread_y = 2.0 * red_y + (block.load(reds, 3, -1) + block.load(reds, 3, 1))
    spread_z = 2.0 * red_z + (block.load(reds, 4, -1) + block.load(reds, 4, 1))
    up_y, down_y = red + red_y, red - red_y
    low_y = (
        (spread + spread_y)
        + geometry.from_low_z(up_y + red_z)
        + geometry.from_high_z(up_y - red_z)
    )
    high_y = (
        (spread - spread_y)
        + geometry.from_low_z(down_y + red_z)
        + geometry.from_high_z(down_y - red_z)
    )
    bounced = (
        block.walls(walls, 3) * red
        - block.walls(walls, 0) * (red_x_up - red)
        - block.walls(walls, 1) * red_y
        - block.walls(walls, 2) * red_z
    )
    red_total = (
        12.0 * red
        + 2.0 * from_x
        + geometry.from_low_z(spread + spread_z)
        + geometry.from_high_z(spread - spread_z)
        + geometry.from_low_y(low_y)
        + geometry.from_high_y(high_y)
        + bounced
    )
    block.store(fields, 10, red_total)


def over_rows(geometry, first, end, size, blocks, stage):
    trip = size * blocks

    def step(index, carry):
        start = jnp.minimum(first + index * trip, end - trip)
        for number in range(blocks):
            row = start + number * size
            stage(Block(geometry, [(row, row, size)], inner=True))
        return carry

    lax.fori_loop(0, (end - first + trip - 1) // trip, step, 0)


def load_kernel(
    tiles_count, density, momentum, stress, red, solid, widths,
    info, spread, packet, mine,
    raw, raw_solid, held_widths, sems,
):
    row_count, flat_count = raw_solid.shape
    own_tiles = flat_count // LANES
    planes = [density] + [momentum.at[axis] for axis in range(3)]
    planes = planes + [stress.at[part] for part in range(6)] + [red]
    copies = [pltpu.make_async_copy(widths, held_widths, sems.at[PLANES])]
    copies.append(pltpu.make_async_copy(solid, raw_solid, sems.at[FIELDS]))
    for index, plane in enumerate(planes):
        copies.append(pltpu.make_async_copy(plane, raw.at[index], sems.at[index]))
    for copy in copies:
        copy.start()
    tiles_index, sub_index = lax.axis_index("tiles"), lax.axis_index("sub")
    low_part = sub_index == 0
    edge_start = pl.multiple_of(jnp.where(low_part, (own_tiles - 1) * LANES, 0), LANES)

    copies[0].wait()
    live = held_widths[tiles_index] * TILE
    info[0] = live
    info[1] = (tiles_index == 0).astype(jnp.int32)
    info[2] = (tiles_index == tiles_count - 1).astype(jnp.int32)
    info[3] = sub_index

    near_cut = lax.broadcasted_iota(jnp.int32, (SUBLANES, LANES), 1) < HALF
    near_cut = near_cut == jnp.logical_not(low_part)
    for index in range(PLANES):
        source = raw_solid if index == FIELDS else raw.at[index]
        copies[1 if index == FIELDS else 2 + index].wait()
        for row in range(0, row_count, SUBLANES):
            rows = pl.ds(row, SUBLANES)
            for tile in range(own_tiles):
                values = source[rows, pl.ds(tile * LANES, LANES)].astype(jnp.float32)
                start = row * SUBLANES + 1 + tile
                spread[index, pl.ds(start, SUBLANES, stride=SUBLANES), :] = values
            if index >= PAIRS:
                values = source[rows, pl.ds(edge_start, LANES)].astype(jnp.float32)
                first = raw[index - PAIRS, rows, pl.ds(edge_start, LANES)]
                both = jnp.where(near_cut, first, pltpu.roll(values, HALF, 1))
                packet[pl.ds((index - PAIRS) * row_count + row, SUBLANES), :] = both

    after = PAIRS * row_count
    ends = (
        (packet, after, jnp.where(low_part, 0, live - FULL), jnp.where(low_part, FULL, live - HALO)),
        (mine, 0, jnp.where(low_part, live - FULL, 0), jnp.where(low_part, live - HALO, FULL)),
    )
    for target, at, full_row, colour_row in ends:
        rows = pl.ds(colour_row * SUBLANES + 1, OWN_TILES)
        target[pl.ds(at, OWN_TILES), :] = 2.0 * spread[10, rows, :] - spread[0, rows, :]
        for index in range(PLANES):
            for extra in range(FULL):
                place = at + (1 + FULL * index + extra) * OWN_TILES
                rows = pl.ds((full_row + extra) * SUBLANES + 1, OWN_TILES)
                target[pl.ds(place, OWN_TILES), :] = spread[index, rows, :]


def load_inputs(arrays, widths, tiles_count):
    row_count, flat_count = arrays[0].shape
    packet_rows = PAIRS * row_count + END_ROWS
    return pl.pallas_call(
        functools.partial(load_kernel, tiles_count),
        out_shape=[
            jax.ShapeDtypeStruct((4,), jnp.int32),
            jax.ShapeDtypeStruct((PLANES, row_count * SUBLANES, LANES), jnp.float32),
            jax.ShapeDtypeStruct((packet_rows, LANES), jnp.float32),
            jax.ShapeDtypeStruct((END_ROWS, LANES), jnp.float32),
        ],
        in_specs=[HBM] * 6,
        out_specs=[SMEM, VMEM, VMEM, VMEM],
        scratch_shapes=[
            pltpu.VMEM((FIELDS, row_count, flat_count), jnp.float32),
            pltpu.VMEM((row_count, flat_count), jnp.int32),
            pltpu.SMEM(widths.shape, jnp.int32),
            pltpu.SemaphoreType.DMA((PLANES + 1,)),
        ],
        compiler_params=pltpu.CompilerParams(vmem_limit_bytes=16 * 1024 * 1024),
        name="load",
    )(*[pltpu.with_memory_space_constraint(array, pltpu.HBM) for array in (*arrays, widths)])


def join_kernel(info, spread, packet, mine, whole, ends):
    low_part = info[3] == 0
    row_count = spread.shape[1] // SUBLANES
    ends[pl.ds(0, END_ROWS), :] = mine[...]
    ends[pl.ds(END_ROWS, END_ROWS), :] = packet[pl.ds(PAIRS * row_count, END_ROWS), :]
    for pair in range(PAIRS):
        for row in range(0, row_count, SUBLANES):
            both = packet[pl.ds(pair * row_count + row, SUBLANES), :]
            start = row * SUBLANES
            for index, values in ((pair, both), (pair + PAIRS, pltpu.roll(both, HALF, 1))):
                below = jnp.where(low_part, 0.0, values)
                above = jnp.where(low_part, values, 0.0)
                whole[index, pl.ds(start, SUBLANES, stride=SUBLANES), :] = below
                whole[index, pl.ds(start + SUBLANES - 1, SUBLANES, stride=SUBLANES), :] = above


def join_parts(info, spread, packet, mine):
    return pl.pallas_call(
        join_kernel,
        out_shape=[
            jax.ShapeDtypeStruct(spread.shape, jnp.float32),
            jax.ShapeDtypeStruct((2 * END_ROWS, LANES), jnp.float32),
        ],
        in_specs=[SMEM, VMEM, VMEM, VMEM],
        out_specs=[VMEM] * 2,
        input_output_aliases={1: 0},
        compiler_params=pltpu.CompilerParams(vmem_limit_bytes=16 * 1024 * 1024),
        name="join",
    )(info, pltpu.with_memory_space_constraint(spread, pltpu.VMEM), packet, mine)


def keep_rows(target, target_index, source, index, rows, size):
    for place, row in enumerate(rows):
        target[target_index, flat_rows(place * size, size), :] = source[
            index, flat_rows(row, size), :
        ]


def collide_rows(geometry, before, whole, first, scratch, moved, reds):
    colours, walls = scratch
    end = geometry.live - first
    over_rows(geometry, first - 1, end + 1, *COLOUR_BLOCK, lambda block: colour_stage(
        block, geometry, before, colours))
    over_rows(geometry, first, end, *COLLIDE_BLOCK, lambda block: collide_stage(
        block, geometry, before, whole, colours, walls, moved, reds))


def arrive_rows(geometry, first, walls, moved, reds, after):
    over_rows(geometry, first, geometry.live - first, *ARRIVE_BLOCK, lambda block: arrive_stage(
        block, geometry, walls, moved, reds, after))


def keep_moved(target, moved, reds, rows):
    for index in range(MOVED):
        keep_rows(target, index, moved, index, rows, 2)
    for index in range(REDS):
        keep_rows(target, MOVED + index, reds, index, rows, 2)


def first_kernel(info, whole, moved_later, reds_later, moved_rim, fields_rim, *scratch):
    colours, walls, moved, reds, fields = scratch
    geometry = Geometry(info, OWN_TILES)
    live = geometry.live
    fill_wall_table(walls, geometry)
    collide_rows(geometry, whole, whole, 1, (colours, walls), moved, reds)
    arrive_rows(geometry, 2, walls, moved, reds, fields)
    keep_moved(moved_rim, moved, reds, (1, live - 3))
    for index in range(FIELDS):
        keep_rows(fields_rim, index, fields, index, (2, live - 4), 2)
    collide_rows(geometry, fields, whole, 3, (colours, walls), moved_later, reds_later)


def tile_copies(pieces, outs, held_row, out_row, sems):
    held, rows = pl.ds(held_row, SUBLANES), pl.ds(out_row, SUBLANES)
    parts = (
        (pieces.at[0, held], outs[0].at[rows]),
        (pieces.at[pl.ds(1, 3), held], outs[1].at[:, rows]),
        (pieces.at[pl.ds(4, 6), held], outs[2].at[:, rows]),
        (pieces.at[10, held], outs[3].at[rows]),
    )
    return [
        pltpu.make_async_copy(source, target, sems.at[number])
        for number, (source, target) in enumerate(parts)
    ]


def gather_tiles(final, row, pieces, held_row):
    for index in range(FIELDS):
        for tile in range(OWN_TILES):
            start = pl.multiple_of(row * SUBLANES, SUBLANES) + 1 + tile
            pieces[index, pl.ds(held_row, SUBLANES), pl.ds(tile * LANES, LANES)] = final[
                index, pl.ds(start, SUBLANES, stride=SUBLANES), :
            ]


def second_kernel(
    info, moved, reds, arrived, density_out, momentum_out, stress_out, red_out,
    moved_rim, final_rim, final, walls, pieces, zeros, sems,
):
    outs = (density_out, momentum_out, stress_out, red_out)
    row_tiles = density_out.shape[0] // SUBLANES
    geometry = Geometry(info, OWN_TILES)
    live = geometry.live
    fill_wall_table(walls, geometry)

    zeros[...] = jnp.zeros(zeros.shape, zeros.dtype)
    dead = {}
    for tile in range(row_tiles):
        dead[tile] = tile_copies(zeros, outs, 0, tile * SUBLANES, sems.at[tile])

        @pl.when(tile * SUBLANES >= live)
        def _():
            for copy in dead[tile]:
                copy.start()

    edge = Block(geometry, [(RIM, RIM, RIM), (live - 2 * RIM, live - 2 * RIM, RIM)], True, [0, RIM])
    arrive_stage(edge, geometry, walls, moved, reds, final_rim)
    keep_moved(moved_rim, moved, reds, (3, live - 5))

    def copies_of(tile):
        row = pl.multiple_of(tile * SUBLANES, SUBLANES)
        return tile_copies(pieces, outs, row, row, sems.at[tile])

    def finish(tile, carry):
        row = pl.multiple_of(tile * SUBLANES, SUBLANES)
        arrive_stage(
            Block(geometry, [(row, row, SUBLANES)], inner=True), geometry, walls, moved, reds, final
        )
        gather_tiles(final, row, pieces, row)
        for copy in copies_of(tile):
            copy.start()
        return carry

    def settle(tile, carry):
        for copy in copies_of(tile):
            copy.wait()
        return carry

    last = live // SUBLANES - 1
    lax.fori_loop(1, last, finish, 0)
    lax.fori_loop(1, last, settle, 0)
    for tile in range(row_tiles):

        @pl.when(tile * SUBLANES >= live)
        def _():
            for copy in dead[tile]:
                copy.wait()


def rim_shape(count, rows):
    return jax.ShapeDtypeStruct((count, rows * SUBLANES, LANES), jnp.float32)


def run_first(info, whole):
    flat = whole.shape[1]
    shapes = [
        jax.ShapeDtypeStruct((MOVED, flat, LANES), jnp.float32),
        jax.ShapeDtypeStruct((REDS, flat, LANES), jnp.float32),
        rim_shape(MOVED + REDS, 4),
        rim_shape(FIELDS, 4),
    ]
    return pl.pallas_call(
        first_kernel,
        out_shape=shapes,
        in_specs=[SMEM, VMEM],
        out_specs=[VMEM] * len(shapes),
        scratch_shapes=[
            pltpu.VMEM((4, flat, LANES), jnp.float32),
            pltpu.VMEM((4, 3 * SUBLANES, LANES), jnp.float32),
            pltpu.VMEM((MOVED, flat, LANES), jnp.float32),
            pltpu.VMEM((REDS, flat, LANES), jnp.float32),
            pltpu.VMEM((FIELDS, flat, LANES), jnp.float32),
        ],
        compiler_params=pltpu.CompilerParams(vmem_limit_bytes=24 * 1024 * 1024),
        cost_estimate=pl.CostEstimate(flops=20_000_000, bytes_accessed=8_000_000, transcendentals=0),
        name="first",
    )(info, whole)


def run_second(info, moved, reds, arrived, arrays):
    flat = moved.shape[1]
    row_count, flat_count = arrays[0].shape
    shapes = [jax.ShapeDtypeStruct(array.shape, jnp.float32) for array in arrays[:4]]
    shapes = shapes + [rim_shape(MOVED + REDS, 4), rim_shape(FIELDS, 2 * RIM)]
    return pl.pallas_call(
        second_kernel,
        out_shape=shapes,
        in_specs=[SMEM, VMEM, VMEM, ANY],
        out_specs=[ANY] * 4 + [VMEM] * 2,
        scratch_shapes=[
            pltpu.VMEM((FIELDS, flat, LANES), jnp.float32),
            pltpu.VMEM((4, 3 * SUBLANES, LANES), jnp.float32),
            pltpu.VMEM((FIELDS, row_count, flat_count), jnp.float32),
            pltpu.VMEM((FIELDS, SUBLANES, flat_count), jnp.float32),
            pltpu.SemaphoreType.DMA((row_count // SUBLANES, 4)),
        ],
        compiler_params=pltpu.CompilerParams(vmem_limit_bytes=24 * 1024 * 1024),
        cost_estimate=pl.CostEstimate(flops=20_000_000, bytes_accessed=8_000_000, transcendentals=0),
        name="second",
    )(info, moved, reds, arrived)


def outer_kernel(
    info, whole, arrived, passed, moved_rim, fields_rim, moved_later_rim, final_rim, *refs,
):
    outs = refs[4:8]
    start_fields, colours, walls, moved, reds, fields, moved_later, reds_later, final = refs[8:17]
    pieces, sems = refs[17:]
    geometry = Geometry(info, OWN_TILES)
    live = geometry.live
    low_part = info[3] == 0
    fill_wall_table(walls, geometry)

    def receive(piece, index, low_row, high_row):
        here = pl.ds(piece * OWN_TILES, OWN_TILES)
        there = pl.ds(END_ROWS + piece * OWN_TILES, OWN_TILES)
        straight, crossed = (arrived[here, :], arrived[there, :]), (passed[there, :], passed[here, :])
        for row, first, second in ((low_row, straight, crossed), (high_row, crossed, straight)):
            own, other = [jnp.where(low_part, one, two) for one, two in zip(first, second)]
            start = row * SUBLANES
            below = jnp.where(low_part, 0.0, other[OWN_TILES - 1 :])
            above = jnp.where(low_part, other[:1], 0.0)
            start_fields[index, pl.ds(start, 1), :] = below
            start_fields[index, pl.ds(start + 1, OWN_TILES), :] = own
            start_fields[index, pl.ds(start + SUBLANES - 1, 1), :] = above

    def spans(first, count):
        mirrored = SLAB - first - count
        return [
            (first - HALO, first, count),
            (live - 2 * RIM + mirrored, SLAB + mirrored, count),
        ]

    for index in range(PLANES):
        for extra in range(FULL):
            receive(1 + FULL * index + extra, index, 1 + extra, 2 * SLAB - HALO + extra)
        start_fields[index, flat_rows(HALO, 2), :] = whole[index, flat_rows(0, 2), :]
        start_fields[index, flat_rows(2 * SLAB - HALO - 2, 2), :] = whole[
            index, flat_rows(live - 2, 2), :
        ]
    receive(0, 10, 0, 2 * SLAB - 1)
    for row in (0, 2 * SLAB - 1):
        start_fields[0, flat_rows(row, 1), :] = jnp.zeros((SUBLANES, LANES), jnp.float32)
        start_fields[10, flat_rows(row, 1), :] = 0.5 * start_fields[10, flat_rows(row, 1), :]

    def place(target, index, source, at, first, size):
        for place, (row, local, count) in enumerate(spans(first, size)):
            target[index, flat_rows(local, size), :] = source[at, flat_rows(place * size, size), :]

    for index in range(MOVED + REDS):
        target, later, at = moved, moved_later, index
        if index >= MOVED:
            target, later, at = reds, reds_later, index - MOVED
        place(target, at, moved_rim, index, HALO + 1, 2)
        place(later, at, moved_later_rim, index, HALO + 3, 2)
    for index in range(FIELDS):
        place(fields, index, fields_rim, index, HALO + 2, 2)
        place(final, index, final_rim, index, HALO + RIM, RIM)

    block = lambda first, count: Block(geometry, spans(first, count))
    colour_stage(block(0, 6), geometry, start_fields, colours)
    collide_stage(block(1, 4), geometry, start_fields, start_fields, colours, walls, moved, reds)
    arrive_stage(block(2, 4), geometry, walls, moved, reds, fields)
    start_fields[PLANES - 1, flat_rows(HALO + 2, 1), :] = whole[PLANES - 1, flat_rows(2, 1), :]
    start_fields[PLANES - 1, flat_rows(2 * SLAB - HALO - 3, 1), :] = whole[
        PLANES - 1, flat_rows(live - 3, 1), :
    ]
    colour_stage(block(2, 6), geometry, fields, colours)
    collide_stage(
        block(3, 4), geometry, fields, start_fields, colours, walls, moved_later, reds_later
    )
    arrive_stage(block(4, 4), geometry, walls, moved_later, reds_later, final)

    copies = []
    for side, row, out_row in ((0, HALO, 0), (1, SLAB, live - SUBLANES)):
        gather_tiles(final, row, pieces, side * SUBLANES)
        out_row = pl.multiple_of(out_row, SUBLANES)
        copies = copies + tile_copies(pieces, outs, side * SUBLANES, out_row, sems.at[side])
    for copy in copies:
        copy.start()
    for copy in copies:
        copy.wait()


def run_outer(info, whole, arrived, passed, rims, outs):
    flat = 2 * SLAB * SUBLANES
    flat_count = outs[0].shape[1]
    return pl.pallas_call(
        outer_kernel,
        out_shape=[jax.ShapeDtypeStruct(out.shape, jnp.float32) for out in outs],
        in_specs=[SMEM] + [VMEM] * 7 + [ANY] * 4,
        out_specs=[ANY] * 4,
        scratch_shapes=[
            pltpu.VMEM((PLANES, flat, LANES), jnp.float32),
            pltpu.VMEM((4, flat, LANES), jnp.float32),
            pltpu.VMEM((4, 3 * SUBLANES, LANES), jnp.float32),
            pltpu.VMEM((MOVED, flat, LANES), jnp.float32),
            pltpu.VMEM((REDS, flat, LANES), jnp.float32),
            pltpu.VMEM((FIELDS, flat, LANES), jnp.float32),
            pltpu.VMEM((MOVED, flat, LANES), jnp.float32),
            pltpu.VMEM((REDS, flat, LANES), jnp.float32),
            pltpu.VMEM((FIELDS, flat, LANES), jnp.float32),
            pltpu.VMEM((FIELDS, 2 * SUBLANES, flat_count), jnp.float32),
            pltpu.SemaphoreType.DMA((2, 4)),
        ],
        input_output_aliases={8: 0, 9: 1, 10: 2, 11: 3},
        compiler_params=pltpu.CompilerParams(vmem_limit_bytes=32 * 1024 * 1024),
        name="outer",
    )(info, whole, arrived, passed, *rims, *outs)


def body(density, momentum, stress, red_density, solid, widths):
    tiles_count = lax.axis_size("tiles")
    arrays = (density, momentum, stress, red_density, solid)
    info, spread, packet, mine = load_inputs(arrays, widths, tiles_count)
    swap = [(0, 1), (1, 0)]
    packet = lax.ppermute(packet, "sub", swap)
    whole, ends = join_parts(info, spread, packet, mine)
    route = [(2 * k, 2 * k + 2) for k in range(tiles_count - 1)]
    route = route + [(2 * k + 3, 2 * k + 1) for k in range(tiles_count - 1)]
    arrived = lax.ppermute(ends, ("tiles", "sub"), route)
    moved, reds, moved_rim, fields_rim = run_first(info, whole)
    arrived = lax.dynamic_update_slice(arrived, fields_rim[0, :1, :1], (END_ROWS - 1, 0))
    passed = lax.ppermute(arrived, "sub", swap)
    results = run_second(info, moved, reds, arrived, arrays)
    rims = (moved_rim, fields_rim) + tuple(results[4:])
    return tuple(run_outer(info, whole, arrived, passed, rims, results[:4]))


def solution(mesh):
    in_specs = (
        P(("groups", "tiles"), "sub"),
        P(None, ("groups", "tiles"), "sub"),
        P(None, ("groups", "tiles"), "sub"),
        P(("groups", "tiles"), "sub"),
        P(("groups", "tiles"), "sub"),
        P("groups"),
    )
    out_specs = (
        P(("groups", "tiles"), "sub"),
        P(None, ("groups", "tiles"), "sub"),
        P(None, ("groups", "tiles"), "sub"),
        P(("groups", "tiles"), "sub"),
    )
    return jax.shard_map(body, mesh=mesh, in_specs=in_specs, out_specs=out_specs, check_vma=False)
```

profile of v0, /device:TPU:0, one launch (start us, length us, event | category | flops | bytes accessed | tf_op | source)
XLA Modules:
  0.0 31.8 jit_solution(6810492878063413709)
XLA Ops:
  0.6 2.6 %load.1 = (s32[4]{0:T(128)S(1)}, f32[12,384,128]{2,1,0:T(8,128)S(1)}, f32[512,128]{1,0:T(8,128)S(1)}, f32[224,128]{1,0:T(8,128)S(1)}) custom-call(f32[48,768]{1,0:T(8,128)} %density.1, f32[3,48,768]{2,1,0:T(8,128)} %momentum.1, f32[6,48,768]{2,1,0:T(8,128)} %stress.1, f32[48,768]{1,0:T(8,128)} %red.1, s32[48,768]{1,0:T(8,128)} %solid.1, s32[8]{0:T(128)} %widths.1), custom_call_target="tpu_custom_call" | custom-call | tf_op jit(solution)/shard_map/load/pallas_call | solution.py:414
  3.2 0.5 %collective-permute-start = (f32[512,128]{1,0:T(8,128)S(1)}, f32[512,128]{1,0:T(8,128)S(1)}, u32[]{:S(2)}, u32[]{:S(2)}) collective-permute-start(f32[512,128]{1,0:T(8,128)S(1)} %get-tuple-element.22), channel_id=1, source_target_pairs={{0,1},{1,0},{2,3},{3,2},{4,5},{5,4},{6,7},{7,6},{8,9},{9,8},{10,11... | collective-permute-start | bytes 786440 | tf_op jit(solution)/shard_map/ppermute | solution.py:751
  3.7 1.2 %collective-permute-done.packet = f32[512,128]{1,0:T(8,128)S(1)} collective-permute-done((f32[512,128]{1,0:T(8,128)S(1)}, f32[512,128]{1,0:T(8,128)S(1)}, u32[]{:S(2)}, u32[]{:S(2)}) %collective-permute-start) | collective-permute-done | bytes 262176 | tf_op jit(solution)/shard_map/ppermute | solution.py:751
  4.9 0.7 %join.1 = (f32[12,384,128]{2,1,0:T(8,128)S(1)}, f32[448,128]{1,0:T(8,128)S(1)}) custom-call(s32[4]{0:T(128)S(1)} %get-tuple-element.20.info, f32[12,384,128]{2,1,0:T(8,128)S(1)} %get-tuple-element.21.spread, f32[512,128]{1,0:T(8,128)S(1)} %collective-permute-done.packet, f32[224,128]{1,0:T(8,128)S(1)} %get-tuple-element.23.mine), custom_call_target="tpu_custom_call", output_to_operand_aliasing={{0}: (1, {})} | custom-call | tf_op jit(solution)/shard_map/join/pallas_call | solution.py:452
  5.6 5.5 %collective-permute-start.1 = (f32[448,128]{1,0:T(8,128)S(1)}, f32[448,128]{1,0:T(8,128)}, u32[]{:S(2)}, u32[]{:S(2)}) collective-permute-start(f32[448,128]{1,0:T(8,128)S(1)} %get-tuple-element.25), channel_id=1, source_target_pairs={{0,2},{2,4},{4,6},{6,8},{8,10},{10,12},{12,14},{3,1},{5,3},{7,5},{... | collective-permute-start | bytes 688136 | tf_op jit(solution)/shard_map/ppermute | solution.py:755
  11.1 7.0 %first.1 = (f32[19,384,128]{2,1,0:T(8,128)S(1)}, f32[5,384,128]{2,1,0:T(8,128)S(1)}, f32[24,32,128]{2,1,0:T(8,128)S(1)}, f32[11,32,128]{2,1,0:T(8,128)S(1)}) custom-call(s32[4]{0:T(128)S(1)} %get-tuple-element.20.info, f32[12,384,128]{2,1,0:T(8,128)S(1)} %get-tuple-element.24.whole), custom_call_target="tpu_custom_call" | custom-call | flops 20000000 | bytes 8000000 | tf_op jit(solution)/shard_map/first/pallas_call | solution.py:596
  18.0 0.0 copy-start
  18.0 1.8 %copy-done = f32[19,384,128]{2,1,0:T(8,128)} copy-done((f32[19,384,128]{2,1,0:T(8,128)}, f32[19,384,128]{2,1,0:T(8,128)S(1)}, u32[]{:S(2)}) %copy-start) | copy-done | bytes 3735576
  19.9 0.0 copy-start.2
  19.9 0.7 %copy-done.2 = f32[24,32,128]{2,1,0:T(8,128)} copy-done((f32[24,32,128]{2,1,0:T(8,128)}, f32[24,32,128]{2,1,0:T(8,128)S(1)}, u32[]{:S(2)}) %copy-start.2) | copy-done | bytes 393240
  20.6 0.5 %slice.3 = f32[1,1,1]{2,1,0:T(1,128)} slice(f32[11,32,128]{2,1,0:T(8,128)S(1)} %get-tuple-element.26.fields_rim), slice={[0:1], [0:1], [0:1]} | slice | bytes 8 | tf_op jit(solution)/shard_map/slice | solution.py:757
  21.1 0.0 collective-permute-done.1
  21.1 1.9 %dynamic_update_slice.3.arrived = f32[448,128]{1,0:T(8,128)} dynamic-update-slice(f32[448,128]{1,0:T(8,128)} %collective-permute-done.1, f32[1,1]{1,0:T(1,128)} %bitcast, s32[]{:T(128)} %constant.0.clone.1, s32[]{:T(128)} %constant.1.clone.1) | dynamic-update-slice | bytes 12 | tf_op jit(solution)/shard_map/dynamic_update_slice | solution.py:757
  23.0 0.0 collective-permute-start.2
  23.0 0.0 copy-start.1
  23.1 2.1 %copy-done.1 = f32[19,384,128]{2,1,0:T(8,128)S(1)} copy-done((f32[19,384,128]{2,1,0:T(8,128)S(1)}, f32[19,384,128]{2,1,0:T(8,128)}, u32[]{:S(2)}) %copy-start.1) | copy-done | bytes 3735576
  25.1 0.0 copy-start.3
  25.1 3.3 %second.1 = (f32[48,768]{1,0:T(8,128)}, f32[3,48,768]{2,1,0:T(8,128)}, f32[6,48,768]{2,1,0:T(8,128)}, f32[48,768]{1,0:T(8,128)}, f32[24,32,128]{2,1,0:T(8,128)S(1)}, /*index=5*/f32[11,64,128]{2,1,0:T(8,128)S(1)}) custom-call(s32[4]{0:T(128)S(1)} %get-tuple-element.20.info, f32[19,384,128]{2,1,0:T(8,128)S(1)} %copy-done.1, ...), custom_call_target="tpu_custom_call" | custom-call | flops 20000000 | bytes 8000000 | tf_op jit(solution)/shard_map/second/pallas_call | solution.py:619
  28.5 0.0 collective-permute-done.2.passed
  28.5 0.0 copy-done.3
  28.5 3.3 %outer.1 = (f32[48,768]{1,0:T(8,128)}, f32[3,48,768]{2,1,0:T(8,128)}, f32[6,48,768]{2,1,0:T(8,128)}, f32[48,768]{1,0:T(8,128)}) custom-call(s32[4]{0:T(128)S(1)} %get-tuple-element.20.info, f32[12,384,128]{2,1,0:T(8,128)S(1)} %get-tuple-element.24.whole, ...), custom_call_target="tpu_custom_call", output_to_operand_aliasing={{0}: (8, {}), {1}: (9, {}), {2}: (10, {}), {3}: (11, {})} | custom-call | tf_op jit(solution)/shard_map/outer/pallas_call | solution.py:722
Async XLA Ops:
  3.2 1.7 %collective-permute-start = (f32[512,128]{1,0:T(8,128)S(1)}, f32[512,128]{1,0:T(8,128)S(1)}, u32[]{:S(2)}, u32[]{:S(2)}) collective-permute-start(f32[512,128]{1,0:T(8,128)S(1)} %get-tuple-element.22), channel_id=1, source_target_pairs={{0,1},{1,0},{2,3},{3,2},{4,5},{5,4},{6,7},{7,6},{8,9},{9,8},{10,11... | collective-permute-start | bytes 786440 | tf_op jit(solution)/shard_map/ppermute | solution.py:751
  5.6 15.6 %collective-permute-start.1 = (f32[448,128]{1,0:T(8,128)S(1)}, f32[448,128]{1,0:T(8,128)}, u32[]{:S(2)}, u32[]{:S(2)}) collective-permute-start(f32[448,128]{1,0:T(8,128)S(1)} %get-tuple-element.25), channel_id=1, source_target_pairs={{0,2},{2,4},{4,6},{6,8},{8,10},{10,12},{12,14},{3,1},{5,3},{7,5},{... | collective-permute-start | bytes 688136 | tf_op jit(solution)/shard_map/ppermute | solution.py:755
  18.0 1.8 %copy-start = (f32[19,384,128]{2,1,0:T(8,128)}, f32[19,384,128]{2,1,0:T(8,128)S(1)}, u32[]{:S(2)}) copy-start(f32[19,384,128]{2,1,0:T(8,128)S(1)} %get-tuple-element.28.moved) | copy-start | bytes 11206660
  19.9 0.8 %copy-start.2 = (f32[24,32,128]{2,1,0:T(8,128)}, f32[24,32,128]{2,1,0:T(8,128)S(1)}, u32[]{:S(2)}) copy-start(f32[24,32,128]{2,1,0:T(8,128)S(1)} %get-tuple-element.27.moved_rim) | copy-start | bytes 1179652
  23.0 5.4 %collective-permute-start.2 = (f32[448,128]{1,0:T(8,128)}, f32[448,128]{1,0:T(8,128)S(1)}, u32[]{:S(2)}, u32[]{:S(2)}) collective-permute-start(f32[448,128]{1,0:T(8,128)} %dynamic_update_slice.3.arrived), channel_id=1, source_target_pairs={{0,1},{1,0},{2,3},{3,2},{4,5},{5,4},{6,7},{7,6},{8,9},{9,8},{10,11... | collective-permute-start | bytes 688136 | tf_op jit(solution)/shard_map/ppermute | solution.py:758
  23.0 2.1 %copy-start.1 = (f32[19,384,128]{2,1,0:T(8,128)S(1)}, f32[19,384,128]{2,1,0:T(8,128)}, u32[]{:S(2)}) copy-start(f32[19,384,128]{2,1,0:T(8,128)} %copy-done) | copy-start | bytes 11206660
  25.1 3.4 %copy-start.3 = (f32[24,32,128]{2,1,0:T(8,128)S(1)}, f32[24,32,128]{2,1,0:T(8,128)}, u32[]{:S(2)}) copy-start(f32[24,32,128]{2,1,0:T(8,128)} %copy-done.2) | copy-start | bytes 1179652
where the time goes:
time: 32.1 us; the launch traced here: 31.8 us
  Pallas kernels  16.8 us (52%)
  local copies, waits for them, and re-layouts  7.07 us (22%)
  starting transfers between devices  6.01 us (19%)
  waiting for transfers between devices  1.17 us (4%)
  between operations  0.69 us (2%)
    pallas_call x1, Pallas kernels, run_first(): pl.pallas_call(first_kernel, out_shape=shapes, in_specs=[SMEM, VMEM], out...  6.96 us
    ppermute x1, starting transfers between devices, body(): arrived = lax.ppermute(ends, ('tiles', 'sub'), route)  5.49 us
    unnamed x8, local copies, waits for them, and re-layouts  4.63 us
    pallas_call x1, Pallas kernels, run_second(): pl.pallas_call(second_kernel, out_shape=shapes, in_specs=[SMEM, VMEM, VME...  3.34 us
    pallas_call x1, Pallas kernels, run_outer(): pl.pallas_call(outer_kernel, out_shape=[jax.ShapeDtypeStruct(out.shape, j...  3.29 us
    pallas_call x1, Pallas kernels, load_inputs(): pl.pallas_call(functools.partial(load_kernel, tiles_count), out_shape=[ja...  2.58 us
    dynamic_update_slice x1, local copies, waits for them, and re-layouts, body(): lax.dynamic_update_slice(arrived, fields_rim[0, :1, :1], (END_ROWS - 1, 0))  1.93 us
    ppermute x1, waiting for transfers between devices, body(): packet = lax.ppermute(packet, 'sub', swap)  1.16 us
  transfers between devices with their start and end apart: 3, of which 1 were waited for; matrix products, arithmetic and copies ran while one was open for 2% of the time, Pallas kernels for 32%

commit v1 on v0

--- a/solution.py
+++ b/solution.py
@@ -24,8 +24,9 @@
 RIM = 4
 SLAB = HALO + 2 * RIM
 OWN_TILES = SUBLANES - 2
-END_COUNT = 1 + FULL * PLANES
-END_ROWS = -(-END_COUNT * OWN_TILES // SUBLANES) * SUBLANES
+GROUP = 4
+PACKED = FULL * PLANES // GROUP * (GROUP - 1)
+END_ROWS = (PACKED + 1) * SUBLANES
 HALF = LANES // 2
 PAIRS = PLANES // 2
 COLOUR_BLOCK = (8, 1)
@@ -91,6 +92,7 @@
         self.spans = spans
         self.store_rows = store_rows or [local for row, local, count in spans]
         rows = [row + extra for row, local, count in spans for extra in range(count)]
+        self.inner = inner
         if inner:
             self.x_low = self.x_high = None
             self.valid = geometry.domain
@@ -170,9 +172,10 @@
     grad_x = block.load(colours, 1, 1) - block.load(colours, 1, -1)
     grad_y = geometry.from_high_y(term_y) - geometry.from_low_y(term_y)
     grad_z = geometry.from_high_z(term_z) - geometry.from_low_z(term_z)
-    grad_x = (grad_x - block.walls(walls, 0) * colour) * (1.0 / 12.0)
-    grad_y = (grad_y - block.walls(walls, 1) * colour) * (1.0 / 12.0)
-    grad_z = (grad_z - block.walls(walls, 2) * colour) * (1.0 / 12.0)
+    if not block.inner:
+        grad_x = grad_x - block.walls(walls, 0) * colour
+    grad_y = grad_y - block.walls(walls, 1) * colour
+    grad_z = grad_z - block.walls(walls, 2) * colour
 
     fluid = block.load(solids, PLANES - 1) == 0.0
     density = block.load(fields, 0)
@@ -181,32 +184,27 @@
     stress = [block.load(fields, 4 + part) for part in range(6)]
     square_xx, square_yy, square_zz = grad_x * grad_x, grad_y * grad_y, grad_z * grad_z
     square = square_xx + square_yy + square_zz
-    inverse = jnp.where(fluid, lax.rsqrt(1.0 + square), 0.0)
-    strength = SURFACE * inverse
-    keep = jnp.where(fluid, relaxing, 1.0)
-    sign = jnp.where(fluid, 1.0, -1.0)
+    inverse = jnp.where(fluid, lax.rsqrt(1.0 + square * (1.0 / 144.0)), 0.0)
     trace = third * square
-    surface = (
-        square_xx - trace,
-        square_yy - trace,
-        square_zz - trace,
-        grad_x * grad_y,
-        grad_x * grad_z,
-        grad_y * grad_z,
-    )
-    pairs = ((0, 0), (1, 1), (2, 2), (0, 1), (0, 2), (1, 2))
-    second = [
-        flux[a] * flux[b] + (keep * before + strength * addend)
-        for (a, b), before, addend in zip(pairs, stress, surface)
+    strength = (SURFACE / (8.0 * 144.0)) * inverse
+    keep = jnp.where(fluid, relaxing / 8.0, 1.0 / 8.0)
+    eighths = [0.125 * part for part in flux]
+    own = [
+        eighths[axis] * flux[axis] + (keep * stress[axis] + strength * (squared - trace))
+        for axis, squared in enumerate((square_xx, square_yy, square_zz))
     ]
-    flux = [sign * part for part in flux]
-    mixing = (SEPARATION * red) * (density - red) * inverse
-    charge = [0.5 * part + mixing * grad for part, grad in zip(flux, (grad_x, grad_y, grad_z))]
-
-    base = (density - 1.5 * (second[0] + second[1] + second[2])) * (1.0 / 36.0)
-    run = [part * (1.0 / 12.0) for part in flux]
-    own = [part * 0.125 for part in second[:3]]
-    cross = [part * 0.25 for part in second[3:]]
+    strength, keep = 2.0 * strength, 2.0 * keep
+    quarters = [2.0 * part for part in eighths[:2]]
+    grads = (grad_x, grad_y, grad_z)
+    cross = [
+        quarters[a] * flux[b] + (keep * stress[3 + plane] + strength * (grads[a] * grads[b]))
+        for plane, (a, b) in enumerate(((0, 1), (0, 2), (1, 2)))
+    ]
+    base = density * (1.0 / 36.0) - third * (own[0] + own[1] + own[2])
+    sign = jnp.where(fluid, 1.0 / 12.0, -1.0 / 12.0)
+    run = [sign * part for part in flux]
+    mixing = ((SEPARATION / 144.0) * red) * ((density - red) * inverse)
+    red_run = [0.5 * part + mixing * grad for part, grad in zip(run, grads)]
     block.store(moved, 0, 12.0 * base)
     straight = [base + part for part in own]
     for axis in range(3):
@@ -224,9 +222,8 @@
         block.store(moved, first + 2, other + against)
         block.store(moved, first + 3, other - against)
 
-    scale = jnp.where(block.valid, 1.0 / 12.0, 0.0)
-    red_base = red * (scale * third)
-    red_run = [part * scale for part in charge]
+    red_base = red * jnp.where(block.valid, 1.0 / 36.0, 0.0)
+    red_run = [jnp.where(block.valid, part, 0.0) for part in red_run]
     block.store(reds, 0, red_base)
     block.store(reds, 1, red_base + red_run[0])
     block.store(reds, 2, red_base - red_run[0])
@@ -266,6 +263,40 @@
         wall = functools.reduce(lambda one, two: one | two, masks)
         return jnp.where(wall, here(opposite), values)
 
+    red = block.load(reds, 0)
+    red_y = block.load(reds, 3)
+    red_z = block.load(reds, 4)
+    from_x = block.load(reds, 1, -1) + block.load(reds, 2, 1)
+    spread = 2.0 * red + from_x
+    spread_y = 2.0 * red_y + (block.load(reds, 3, -1) + block.load(reds, 3, 1))
+    spread_z = 2.0 * red_z + (block.load(reds, 4, -1) + block.load(reds, 4, 1))
+    up_y, down_y = red + red_y, red - red_y
+    low_y = (
+        (spread + spread_y)
+        + geometry.from_low_z(up_y + red_z)
+        + geometry.from_high_z(up_y - red_z)
+    )
+    high_y = (
+        (spread - spread_y)
+        + geometry.from_low_z(down_y + red_z)
+        + geometry.from_high_z(down_y - red_z)
+    )
+    bounced = (
+        block.walls(walls, 3) * red
+        - block.walls(walls, 1) * red_y
+        - block.walls(walls, 2) * red_z
+    )
+    if not block.inner:
+        bounced = bounced - block.walls(walls, 0) * (block.load(reds, 1) - red)
+    red_total = (
+        12.0 * red
+        + 2.0 * from_x
+        + geometry.from_low_z(spread + spread_z)
+        + geometry.from_high_z(spread - spread_z)
+        + geometry.from_low_y(low_y)
+        + geometry.from_high_y(high_y)
+        + bounced
+    )
     rest = here(0)
     sums, diffs = [], []
     for axis in range(3):
@@ -299,41 +330,6 @@
         block.store(fields, 4 + axis, sums[axis] - shared - diffs[axis] * diffs[axis])
     for plane, (a, b) in enumerate(((0, 1), (0, 2), (1, 2))):
         block.store(fields, 7 + plane, cross[plane] - diffs[a] * diffs[b])
-
-    red = block.load(reds, 0)
-    red_x_up = block.load(reds, 1)
-    red_y = block.load(reds, 3)
-    red_z = block.load(reds, 4)
-    from_x = block.load(reds, 1, -1) + block.load(reds, 2, 1)
-    spread = 2.0 * red + from_x
-    spread_y = 2.0 * red_y + (block.load(reds, 3, -1) + block.load(reds, 3, 1))
-    spread_z = 2.0 * red_z + (block.load(reds, 4, -1) + block.load(reds, 4, 1))
-    up_y, down_y = red + red_y, red - red_y
-    low_y = (
-        (spread + spread_y)
-        + geometry.from_low_z(up_y + red_z)
-        + geometry.from_high_z(up_y - red_z)
-    )
-    high_y = (
-        (spread - spread_y)
-        + geometry.from_low_z(down_y + red_z)
-        + geometry.from_high_z(down_y - red_z)
-    )
-    bounced = (
-        block.walls(walls, 3) * red
-        - block.walls(walls, 0) * (red_x_up - red)
-        - block.walls(walls, 1) * red_y
-        - block.walls(walls, 2) * red_z
-    )
-    red_total = (
-        12.0 * red
-        + 2.0 * from_x
-        + geometry.from_low_z(spread + spread_z)
-        + geometry.from_high_z(spread - spread_z)
-        + geometry.from_low_y(low_y)
-        + geometry.from_high_y(high_y)
-        + bounced
-    )
     block.store(fields, 10, red_total)
 
 
@@ -348,6 +344,33 @@
         return carry
 
     lax.fori_loop(0, (end - first + trip - 1) // trip, step, 0)
+
+
+def block_tiles():
+    return lax.broadcasted_iota(jnp.int32, (SUBLANES, LANES), 0)
+
+
+def roll_tiles(block, amount):
+    return pltpu.roll(block, amount % SUBLANES, 0)
+
+
+def pack_blocks(blocks):
+    tiles, rest = block_tiles(), blocks[GROUP - 1]
+    packed = []
+    for number, block in enumerate(blocks[: GROUP - 1]):
+        low, high = 2 * number + 1, 2 * number + 2
+        block = jnp.where(tiles == 0, roll_tiles(rest, -low), block)
+        packed.append(jnp.where(tiles == SUBLANES - 1, roll_tiles(rest, SUBLANES - 1 - high), block))
+    return packed
+
+
+def unpack_blocks(packed):
+    tiles, rest = block_tiles(), None
+    for number, block in enumerate(packed):
+        low, high = 2 * number + 1, 2 * number + 2
+        part = jnp.where(tiles == low, roll_tiles(block, low), roll_tiles(block, high - SUBLANES + 1))
+        rest = part if rest is None else jnp.where(tiles >= low, part, rest)
+    return list(packed) + [rest]
 
 
 def load_kernel(
@@ -357,12 +380,15 @@
 ):
     row_count, flat_count = raw_solid.shape
     own_tiles = flat_count // LANES
-    planes = [density] + [momentum.at[axis] for axis in range(3)]
-    planes = planes + [stress.at[part] for part in range(6)] + [red]
-    copies = [pltpu.make_async_copy(widths, held_widths, sems.at[PLANES])]
-    copies.append(pltpu.make_async_copy(solid, raw_solid, sems.at[FIELDS]))
-    for index, plane in enumerate(planes):
-        copies.append(pltpu.make_async_copy(plane, raw.at[index], sems.at[index]))
+    copies = [
+        pltpu.make_async_copy(widths, held_widths, sems.at[0]),
+        pltpu.make_async_copy(density, raw.at[0], sems.at[1]),
+        pltpu.make_async_copy(momentum, raw.at[pl.ds(1, 3)], sems.at[2]),
+        pltpu.make_async_copy(red, raw.at[10], sems.at[3]),
+        pltpu.make_async_copy(solid, raw_solid, sems.at[4]),
+        pltpu.make_async_copy(stress.at[pl.ds(0, 3)], raw.at[pl.ds(4, 3)], sems.at[5]),
+        pltpu.make_async_copy(stress.at[pl.ds(3, 3)], raw.at[pl.ds(7, 3)], sems.at[6]),
+    ]
     for copy in copies:
         copy.start()
     tiles_index, sub_index = lax.axis_index("tiles"), lax.axis_index("sub")
@@ -378,20 +404,26 @@
 
     near_cut = lax.broadcasted_iota(jnp.int32, (SUBLANES, LANES), 1) < HALF
     near_cut = near_cut == jnp.logical_not(low_part)
-    for index in range(PLANES):
+    ready = {0: copies[1], 1: copies[2], 10: copies[3], 11: copies[4], 4: copies[5], 7: copies[6]}
+    for index in (0, 1, 2, 3, 10, 11, 4, 5, 6, 7, 8, 9):
         source = raw_solid if index == FIELDS else raw.at[index]
-        copies[1 if index == FIELDS else 2 + index].wait()
+        if index in ready:
+            ready[index].wait()
         for row in range(0, row_count, SUBLANES):
             rows = pl.ds(row, SUBLANES)
             for tile in range(own_tiles):
                 values = source[rows, pl.ds(tile * LANES, LANES)].astype(jnp.float32)
                 start = row * SUBLANES + 1 + tile
                 spread[index, pl.ds(start, SUBLANES, stride=SUBLANES), :] = values
-            if index >= PAIRS:
-                values = source[rows, pl.ds(edge_start, LANES)].astype(jnp.float32)
-                first = raw[index - PAIRS, rows, pl.ds(edge_start, LANES)]
-                both = jnp.where(near_cut, first, pltpu.roll(values, HALF, 1))
-                packet[pl.ds((index - PAIRS) * row_count + row, SUBLANES), :] = both
+
+    edges = pl.ds(edge_start, LANES)
+    for pair in range(PAIRS):
+        later = raw_solid if pair + PAIRS == FIELDS else raw.at[pair + PAIRS]
+        for row in range(0, row_count, SUBLANES):
+            rows = pl.ds(row, SUBLANES)
+            beside = pltpu.roll(later[rows, edges].astype(jnp.float32), HALF, 1)
+            both = jnp.where(near_cut, raw[pair, rows, edges], beside)
+            packet[pl.ds(pair * row_count + row, SUBLANES), :] = both
 
     after = PAIRS * row_count
     ends = (
@@ -399,13 +431,17 @@
         (mine, 0, jnp.where(low_part, live - FULL, 0), jnp.where(low_part, live - HALO, FULL)),
     )
     for target, at, full_row, colour_row in ends:
-        rows = pl.ds(colour_row * SUBLANES + 1, OWN_TILES)
-        target[pl.ds(at, OWN_TILES), :] = 2.0 * spread[10, rows, :] - spread[0, rows, :]
-        for index in range(PLANES):
-            for extra in range(FULL):
-                place = at + (1 + FULL * index + extra) * OWN_TILES
-                rows = pl.ds((full_row + extra) * SUBLANES + 1, OWN_TILES)
-                target[pl.ds(place, OWN_TILES), :] = spread[index, rows, :]
+        rows = flat_rows(colour_row, 1)
+        place = pl.ds(at + PACKED * SUBLANES, SUBLANES)
+        target[place, :] = 2.0 * spread[10, rows, :] - spread[0, rows, :]
+        for group in range(FULL * PLANES // GROUP):
+            blocks = []
+            for number in range(group * GROUP, (group + 1) * GROUP):
+                index, extra = divmod(number, FULL)
+                blocks.append(spread[index, flat_rows(full_row + extra, 1), :])
+            for number, block in enumerate(pack_blocks(blocks)):
+                place = at + (group * (GROUP - 1) + number) * SUBLANES
+                target[pl.ds(place, SUBLANES), :] = block
 
 
 def load_inputs(arrays, widths, tiles_count):
@@ -425,7 +461,7 @@
             pltpu.VMEM((FIELDS, row_count, flat_count), jnp.float32),
             pltpu.VMEM((row_count, flat_count), jnp.int32),
             pltpu.SMEM(widths.shape, jnp.int32),
-            pltpu.SemaphoreType.DMA((PLANES + 1,)),
+            pltpu.SemaphoreType.DMA((7,)),
         ],
         compiler_params=pltpu.CompilerParams(vmem_limit_bytes=16 * 1024 * 1024),
         name="load",
@@ -634,6 +670,22 @@
     )(info, moved, reds, arrived)
 
 
+def follow_kernel(ends, kept, out):
+    out[pl.ds(PACKED * SUBLANES, 1), :] = jnp.zeros((1, LANES), jnp.float32)
+
+
+def follow(ends, kept):
+    return pl.pallas_call(
+        follow_kernel,
+        out_shape=jax.ShapeDtypeStruct(ends.shape, jnp.float32),
+        in_specs=[VMEM, ANY],
+        out_specs=VMEM,
+        input_output_aliases={0: 0},
+        compiler_params=pltpu.CompilerParams(vmem_limit_bytes=8 * 1024 * 1024),
+        name="follow",
+    )(pltpu.with_memory_space_constraint(ends, pltpu.VMEM), kept)
+
+
 def outer_kernel(
     info, whole, arrived, passed, moved_rim, fields_rim, moved_later_rim, final_rim, *refs,
 ):
@@ -645,18 +697,27 @@
     low_part = info[3] == 0
     fill_wall_table(walls, geometry)
 
-    def receive(piece, index, low_row, high_row):
-        here = pl.ds(piece * OWN_TILES, OWN_TILES)
-        there = pl.ds(END_ROWS + piece * OWN_TILES, OWN_TILES)
-        straight, crossed = (arrived[here, :], arrived[there, :]), (passed[there, :], passed[here, :])
-        for row, first, second in ((low_row, straight, crossed), (high_row, crossed, straight)):
-            own, other = [jnp.where(low_part, one, two) for one, two in zip(first, second)]
-            start = row * SUBLANES
-            below = jnp.where(low_part, 0.0, other[OWN_TILES - 1 :])
-            above = jnp.where(low_part, other[:1], 0.0)
-            start_fields[index, pl.ds(start, 1), :] = below
-            start_fields[index, pl.ds(start + 1, OWN_TILES), :] = own
-            start_fields[index, pl.ds(start + SUBLANES - 1, 1), :] = above
+    def ends_of(ref, half):
+        blocks = []
+        for group in range(FULL * PLANES // GROUP):
+            first = half * (PACKED + 1) + group * (GROUP - 1)
+            packed = [ref[pl.ds((first + k) * SUBLANES, SUBLANES), :] for k in range(GROUP - 1)]
+            blocks = blocks + unpack_blocks(packed)
+        last = half * (PACKED + 1) + PACKED
+        return blocks + [ref[pl.ds(last * SUBLANES, SUBLANES), :]]
+
+    tiles = block_tiles()
+    middle = (tiles >= 1) & (tiles <= OWN_TILES)
+    inside = geometry.domain[0]
+
+    def widened(own, other):
+        beside = jnp.where(tiles == 0, roll_tiles(other, -OWN_TILES), roll_tiles(other, OWN_TILES))
+        return jnp.where(inside, jnp.where(middle, own, beside), 0.0)
+
+    straight = [widened(*pair) for pair in zip(ends_of(arrived, 0), ends_of(arrived, 1))]
+    crossed = [widened(*pair) for pair in zip(ends_of(passed, 1), ends_of(passed, 0))]
+    below = [jnp.where(low_part, *pair) for pair in zip(straight, crossed)]
+    above = [jnp.where(low_part, *pair) for pair in zip(crossed, straight)]
 
     def spans(first, count):
         mirrored = SLAB - first - count
@@ -667,15 +728,16 @@
 
     for index in range(PLANES):
         for extra in range(FULL):
-            receive(1 + FULL * index + extra, index, 1 + extra, 2 * SLAB - HALO + extra)
+            number = FULL * index + extra
+            start_fields[index, flat_rows(1 + extra, 1), :] = below[number]
+            start_fields[index, flat_rows(2 * SLAB - HALO + extra, 1), :] = above[number]
         start_fields[index, flat_rows(HALO, 2), :] = whole[index, flat_rows(0, 2), :]
         start_fields[index, flat_rows(2 * SLAB - HALO - 2, 2), :] = whole[
             index, flat_rows(live - 2, 2), :
         ]
-    receive(0, 10, 0, 2 * SLAB - 1)
-    for row in (0, 2 * SLAB - 1):
+    for row, colour in ((0, below[-1]), (2 * SLAB - 1, above[-1])):
         start_fields[0, flat_rows(row, 1), :] = jnp.zeros((SUBLANES, LANES), jnp.float32)
-        start_fields[10, flat_rows(row, 1), :] = 0.5 * start_fields[10, flat_rows(row, 1), :]
+        start_fields[10, flat_rows(row, 1), :] = 0.5 * colour
 
     def place(target, index, source, at, first, size):
         for place, (row, local, count) in enumerate(spans(first, size)):
@@ -754,7 +816,7 @@
     route = route + [(2 * k + 3, 2 * k + 1) for k in range(tiles_count - 1)]
     arrived = lax.ppermute(ends, ("tiles", "sub"), route)
     moved, reds, moved_rim, fields_rim = run_first(info, whole)
-    arrived = lax.dynamic_update_slice(arrived, fields_rim[0, :1, :1], (END_ROWS - 1, 0))
+    arrived = follow(arrived, fields_rim)
     passed = lax.ppermute(arrived, "sub", swap)
     results = run_second(info, moved, reds, arrived, arrays)
     rims = (moved_rim, fields_rim) + tuple(results[4:])

time: 32.1 us -> 22.6 us (0.70)
  the two profiles are of different devices: /device:TPU:0 before, /device:TPU:5 now
where the time goes in v1:
time: 22.6 us; the launch traced here: 22.4 us
  Pallas kernels  16 us (71%)
  starting transfers between devices  4.61 us (20%)
  waiting for transfers between devices  1.17 us (5%)
  between operations  0.7 us (3%)
    pallas_call x1, Pallas kernels, run_first(): pl.pallas_call(first_kernel, out_shape=shapes, in_specs=[SMEM, VMEM], out...  6.87 us
    pallas_call x1, Pallas kernels, run_second(): pl.pallas_call(second_kernel, out_shape=shapes, in_specs=[SMEM, VMEM, VME...  3.37 us
    pallas_call x1, Pallas kernels, run_outer(): pl.pallas_call(outer_kernel, out_shape=[jax.ShapeDtypeStruct(out.shape, j...  2.9 us
    pallas_call x1, Pallas kernels, load_inputs(): pl.pallas_call(functools.partial(load_kernel, tiles_count), out_shape=[ja...  2.18 us
    ppermute x1, starting transfers between devices, body(): passed = lax.ppermute(arrived, 'sub', swap)  1.95 us
    ppermute x1, starting transfers between devices, body(): arrived = lax.ppermute(ends, ('tiles', 'sub'), route)  1.92 us
    ppermute x1, waiting for transfers between devices, body(): packet = lax.ppermute(packet, 'sub', swap)  1.16 us
    ppermute x1, starting transfers between devices, body(): packet = lax.ppermute(packet, 'sub', swap)  0.74 us
  transfers between devices with their start and end apart: 3, of which 1 were waited for; matrix products, arithmetic and copies ran while one was open for 0% of the time, Pallas kernels for 46%

profile of v1, /device:TPU:5, one launch (start us, length us, event | category | flops | bytes accessed | tf_op | source)
XLA Modules:
  0.0 22.4 jit_solution(7653032197634534962)
XLA Ops:
  0.6 2.2 %load.1 = (s32[4]{0:T(128)S(1)}, f32[12,384,128]{2,1,0:T(8,128)S(1)}, f32[512,128]{1,0:T(8,128)S(1)}, f32[224,128]{1,0:T(8,128)S(1)}) custom-call(f32[48,768]{1,0:T(8,128)} %density.1, f32[3,48,768]{2,1,0:T(8,128)} %momentum.1, f32[6,48,768]{2,1,0:T(8,128)} %stress.1, f32[48,768]{1,0:T(8,128)} %red.1, s32[48,768]{1,0:T(8,128)} %solid.1, s32[8]{0:T(128)} %widths.1), custom_call_target="tpu_custom_call" | custom-call | tf_op jit(solution)/shard_map/load/pallas_call | solution.py:450
  2.8 0.7 %collective-permute-start = (f32[512,128]{1,0:T(8,128)S(1)}, f32[512,128]{1,0:T(8,128)S(1)}, u32[]{:S(2)}, u32[]{:S(2)}) collective-permute-start(f32[512,128]{1,0:T(8,128)S(1)} %get-tuple-element.22), channel_id=1, source_target_pairs={{0,1},{1,0},{2,3},{3,2},{4,5},{5,4},{6,7},{7,6},{8,9},{9,8},{10,11... | collective-permute-start | bytes 786440 | tf_op jit(solution)/shard_map/ppermute | solution.py:813
  3.6 1.2 %collective-permute-done.packet = f32[512,128]{1,0:T(8,128)S(1)} collective-permute-done((f32[512,128]{1,0:T(8,128)S(1)}, f32[512,128]{1,0:T(8,128)S(1)}, u32[]{:S(2)}, u32[]{:S(2)}) %collective-permute-start) | collective-permute-done | bytes 262176 | tf_op jit(solution)/shard_map/ppermute | solution.py:813
  4.7 0.7 %join.1 = (f32[12,384,128]{2,1,0:T(8,128)S(1)}, f32[448,128]{1,0:T(8,128)S(1)}) custom-call(s32[4]{0:T(128)S(1)} %get-tuple-element.20.info, f32[12,384,128]{2,1,0:T(8,128)S(1)} %get-tuple-element.21.spread, f32[512,128]{1,0:T(8,128)S(1)} %collective-permute-done.packet, f32[224,128]{1,0:T(8,128)S(1)} %get-tuple-element.23.mine), custom_call_target="tpu_custom_call", output_to_operand_aliasing={{0}: (1, {})} | custom-call | tf_op jit(solution)/shard_map/join/pallas_call | solution.py:488
  5.4 1.9 %collective-permute-start.1 = (f32[448,128]{1,0:T(8,128)S(1)}, f32[448,128]{1,0:T(8,128)S(1)}, u32[]{:S(2)}, u32[]{:S(2)}) collective-permute-start(f32[448,128]{1,0:T(8,128)S(1)} %get-tuple-element.25), channel_id=1, source_target_pairs={{0,2},{2,4},{4,6},{6,8},{8,10},{10,12},{12,14},{3,1},{5,3},{7,5},{... | collective-permute-start | bytes 688136 | tf_op jit(solution)/shard_map/ppermute | solution.py:817
  7.3 6.9 %first.1 = (f32[19,384,128]{2,1,0:T(8,128)S(1)}, f32[5,384,128]{2,1,0:T(8,128)S(1)}, f32[24,32,128]{2,1,0:T(8,128)S(1)}, f32[11,32,128]{2,1,0:T(8,128)S(1)}) custom-call(s32[4]{0:T(128)S(1)} %get-tuple-element.20.info, f32[12,384,128]{2,1,0:T(8,128)S(1)} %get-tuple-element.24.whole), custom_call_target="tpu_custom_call" | custom-call | flops 20000000 | bytes 8000000 | tf_op jit(solution)/shard_map/first/pallas_call | solution.py:632
  14.2 0.0 collective-permute-done.1.ends
  14.2 1.9 %collective-permute-start.2 = (f32[448,128]{1,0:T(8,128)S(1)}, f32[448,128]{1,0:T(8,128)S(1)}, u32[]{:S(2)}, u32[]{:S(2)}) collective-permute-start(f32[448,128]{1,0:T(8,128)S(1)} %follow.1.arrived), channel_id=1, source_target_pairs={{0,1},{1,0},{2,3},{3,2},{4,5},{5,4},{6,7},{7,6},{8,9},{9,8},{10,11... | collective-permute-start | bytes 688136 | tf_op jit(solution)/shard_map/ppermute | solution.py:820
  16.2 3.4 %second.1 = (f32[48,768]{1,0:T(8,128)}, f32[3,48,768]{2,1,0:T(8,128)}, f32[6,48,768]{2,1,0:T(8,128)}, f32[48,768]{1,0:T(8,128)}, f32[24,32,128]{2,1,0:T(8,128)S(1)}, /*index=5*/f32[11,64,128]{2,1,0:T(8,128)S(1)}) custom-call(s32[4]{0:T(128)S(1)} %get-tuple-element.20.info, f32[19,384,128]{2,1,0:T(8,128)S(1)} %get-tuple-element.28.moved, ...), custom_call_target="tpu_custom_call" | custom-call | flops 20000000 | bytes 8000000 | tf_op jit(solution)/shard_map/second/pallas_call | solution.py:655
  19.5 0.0 collective-permute-done.2.passed
  19.5 2.9 %outer.1 = (f32[48,768]{1,0:T(8,128)}, f32[3,48,768]{2,1,0:T(8,128)}, f32[6,48,768]{2,1,0:T(8,128)}, f32[48,768]{1,0:T(8,128)}) custom-call(s32[4]{0:T(128)S(1)} %get-tuple-element.20.info, f32[12,384,128]{2,1,0:T(8,128)S(1)} %get-tuple-element.24.whole, ...), custom_call_target="tpu_custom_call", output_to_operand_aliasing={{0}: (8, {}), {1}: (9, {}), {2}: (10, {}), {3}: (11, {})} | custom-call | tf_op jit(solution)/shard_map/outer/pallas_call | solution.py:784
  (1 shorter events, 0.0 us)
Async XLA Ops:
  2.8 1.9 %collective-permute-start = (f32[512,128]{1,0:T(8,128)S(1)}, f32[512,128]{1,0:T(8,128)S(1)}, u32[]{:S(2)}, u32[]{:S(2)}) collective-permute-start(f32[512,128]{1,0:T(8,128)S(1)} %get-tuple-element.22), channel_id=1, source_target_pairs={{0,1},{1,0},{2,3},{3,2},{4,5},{5,4},{6,7},{7,6},{8,9},{9,8},{10,11... | collective-permute-start | bytes 786440 | tf_op jit(solution)/shard_map/ppermute | solution.py:813
  5.4 8.8 %collective-permute-start.1 = (f32[448,128]{1,0:T(8,128)S(1)}, f32[448,128]{1,0:T(8,128)S(1)}, u32[]{:S(2)}, u32[]{:S(2)}) collective-permute-start(f32[448,128]{1,0:T(8,128)S(1)} %get-tuple-element.25), channel_id=1, source_target_pairs={{0,2},{2,4},{4,6},{6,8},{8,10},{10,12},{12,14},{3,1},{5,3},{7,5},{... | collective-permute-start | bytes 688136 | tf_op jit(solution)/shard_map/ppermute | solution.py:817
  14.2 5.3 %collective-permute-start.2 = (f32[448,128]{1,0:T(8,128)S(1)}, f32[448,128]{1,0:T(8,128)S(1)}, u32[]{:S(2)}, u32[]{:S(2)}) collective-permute-start(f32[448,128]{1,0:T(8,128)S(1)} %follow.1.arrived), channel_id=1, source_target_pairs={{0,1},{1,0},{2,3},{3,2},{4,5},{5,4},{6,7},{7,6},{8,9},{9,8},{10,11... | collective-permute-start | bytes 688136 | tf_op jit(solution)/shard_map/ppermute | solution.py:820
